TPU v7x, 32 devices: a whole 2x2x4 slice. The times are simulated.
32 devices in a mesh: wide: 32 (over z, y, x, core), narrow: 1.
Axes of the slice: x: 2, y: 2, z: 4, core: 2. Of those that a mesh axis runs over, the one named last changes fastest.
Arguments:
- field: float32 [256, 44, 512], P('wide', 'narrow')
- sketch_one: float32 [512, 128], replicated, may hold values from -6 to 6
- sketch_two: float32 [256, 128], replicated, may hold values from -6 to 6
- ranks: int32 [2], replicated, may hold values from 64 to 128, as said below
Outputs:
- core: float32 [128, 44, 128], P('wide', 'narrow')
Inputs may be any that keep to these rules, and one draw needn't show every extreme that they name: One of the two ranks equals 128.
All inputs are finite; a program needn't handle non-finite values.
Results may differ from a plain program's by a relative error of at most 0.00022.
Values sent between devices are 32-bit elements; how exact they have to be, the bound alone decides.
A program may use at most 64 MiB of HBM per device.

v0:
```python
import jax
import jax.numpy as jnp
from jax import lax
from jax.sharding import PartitionSpec as P


def combine(partial_sum):
    return lax.psum(partial_sum, ("wide", "narrow"))


def make_basis(local, sketch, rank):
    highest = lax.Precision.HIGHEST
    keep = (jnp.arange(sketch.shape[1]) < rank).astype(jnp.float32)
    masked = sketch * keep
    partial_gram = jnp.einsum("akn,akm->nm", local, local, precision=highest)
    sketched = jnp.dot(combine(partial_gram), masked, precision=highest)
    inner = jnp.dot(sketched.T, sketched, precision=highest) + jnp.diag(1.0 - keep)
    lower = jnp.linalg.cholesky(inner)
    return jax.scipy.linalg.solve_triangular(lower, sketched.T, lower=True)


def per_device(field, sketch_one, sketch_two, ranks):
    highest = lax.Precision.HIGHEST
    basis_one = make_basis(field, sketch_one, ranks[0])
    core_one = jnp.einsum("rn,ykn->rky", basis_one, field, precision=highest)
    regrouped = lax.all_to_all(core_one, "wide", split_axis=0, concat_axis=2, tiled=True)
    basis_two = make_basis(regrouped, sketch_two, ranks[1])
    return jnp.einsum("sn,rkn->rks", basis_two, regrouped, precision=highest)


def solution(mesh):
    return jax.shard_map(
        per_device,
        mesh=mesh,
        in_specs=(P("wide", "narrow", None), P(), P(), P()),
        out_specs=P("wide", "narrow", None),
        check_vma=False,
    )
```

profile of v0, /device:TPU:0, one launch (start us, length us, event | category | flops | bytes accessed | tf_op | source)
XLA Modules:
  0.0 346.2 jit_solution(5141929274860126565)
XLA Ops:
  6.5 1.1 copy-done
  7.6 2.9 convolution_bitcast_fusion
  10.6 0.6 copy-done.3
  11.2 0.6 fusion.20
  11.8 0.6 compare_convert_fusion.1
  12.4 0.6 broadcast_subtract_fusion.1
  13.0 132.1 %all-reduce.3.cloned.1.call-done = f32[512,512]{1,0:T(8,128)} async-done(((f32[512,512]{1,0:T(8,128)}), f32[512,512]{1,0:T(8,128)}) %all-reduce.3.cloned.1.call-update) | async-done | bytes 1048592 | tf_op jit(solution)/shard_map/psum | solution.py:8
  145.2 2.2 fusion.6
  147.4 0.6 convolution_add_fusion.1
  148.2 11.7 %cholesky.44 = f32[128,128]{1,0:T(8,128)S(1)} custom-call(f32[128,128]{1,0:T(8,128)S(1)} %copy.22), custom_call_target="Cholesky" | custom-call | tf_op jit(solution)/shard_map/jit(cholesky)/cholesky | solution.py:18
  159.9 0.7 compare_reduce_fusion.1
  160.7 0.7 fusion.11
  161.4 9.8 %custom-call.10 = f32[1,128,128]{1,2,0:T(8,128)S(1)} custom-call(f32[1,128,128]{2,1,0:T(8,128)S(1)} %fusion.11), custom_call_target="InvertDiagBlocksLowerTriangular" | custom-call | tf_op jit(solution)/shard_map/jit(_solve_triangular)/triangular_solve | solution.py:19
  171.2 0.4 convolution_bitcast_fusion.2
  171.6 1.1 convolution_bitcast_fusion.3
  172.9 0.6 reshape.39
  173.6 12.1 %all_to_all.18 = f32[32,1,1408]{2,1,0:T(1,128)S(1)} all-to-all(f32[32,1,1408]{2,1,0:T(1,128)S(1)} %reshape.39), channel_id=1, replica_groups=mesh['wide'=32,'narrow'=1] {'wide'}, dimensions={0} | all-to-all | bytes 360448 | tf_op jit(solution)/shard_map/all_to_all | solution.py:26
  185.7 0.6 broadcast.90
  186.3 1.1 reduce.4
  187.4 0.7 reshape.40
  188.1 1.3 convolution_bitcast_fusion.1
  189.4 0.7 compare_convert_fusion
  190.1 0.7 broadcast_subtract_fusion
  190.8 121.8 %all-reduce.5.cloned.1.call-done = f32[256,256]{1,0:T(8,128)} async-done(((f32[256,256]{1,0:T(8,128)}), f32[256,256]{1,0:T(8,128)}) %all-reduce.5.cloned.1.call-update) | async-done | bytes 262160 | tf_op jit(solution)/shard_map/psum | solution.py:8
  312.6 1.3 fusion.8
  313.9 0.4 convolution_add_fusion
  314.5 11.7 %cholesky.55 = f32[128,128]{1,0:T(8,128)S(1)} custom-call(f32[128,128]{1,0:T(8,128)S(1)} %copy.29), custom_call_target="Cholesky" | custom-call | tf_op jit(solution)/shard_map/jit(cholesky)/cholesky | solution.py:18
  326.3 0.6 compare_reduce_fusion
  326.9 0.7 fusion.12
  327.6 9.8 %custom-call.11 = f32[1,128,128]{1,2,0:T(8,128)S(1)} custom-call(f32[1,128,128]{2,1,0:T(8,128)S(1)} %fusion.12), custom_call_target="InvertDiagBlocksLowerTriangular" | custom-call | tf_op jit(solution)/shard_map/jit(_solve_triangular)/triangular_solve | solution.py:19
  337.7 1.0 fusion.1
  338.7 0.7 copy.31
  (20 shorter events, 1.1 us)
Async XLA Ops:
  6.5 1.1 copy-start
  6.5 138.6 %all-reduce.3.cloned.1.call-start = ((), (), s32[]{:S(2)}) async-start(), calls=%async_computation.1 | async-start | bytes 2097152 | tf_op jit(solution)/shard_map/psum | solution.py:8
  10.5 0.7 copy-start.3
  10.5 134.6 %copy-start.1 = (f32[512,128]{1,0:T(8,128)S(1)}, f32[512,128]{1,0:T(8,128)}, u32[]{:S(2)}) copy-start(f32[512,128]{1,0:T(8,128)} %param.6) | copy-start | bytes 786436
  10.6 302.0 %all-reduce.5.cloned.1.call-start = ((), (), s32[]{:S(2)}) async-start(), calls=%async_computation.2 | async-start | bytes 524288 | tf_op jit(solution)/shard_map/psum | solution.py:8
  189.4 123.2 %copy-start.2 = (f32[256,128]{1,0:T(8,128)S(1)}, f32[256,128]{1,0:T(8,128)}, u32[]{:S(2)}) copy-start(f32[256,128]{1,0:T(8,128)} %param.7) | copy-start | bytes 393220
Sparse Core Ops, SparseCore 0:
  12.5 132.5 all-reduce.2
  189.5 122.9 all-reduce.4
where the time goes:
time: 347 us; the launch traced here: 346 us
  waiting for transfers between devices  254 us (73%)
  other arithmetic  49.5 us (14%)
  between operations  13.6 us (4%)
  blocking collectives  12.1 us (3%)
  matrix products  11.5 us (3%)
  local copies, waits for them, and re-layouts  5.47 us (2%)
    psum x2, waiting for transfers between devices, combine(): return lax.psum(partial_sum, ('wide', 'narrow'))  254 us
    another operation x6, other arithmetic, make_basis(): lower = jnp.linalg.cholesky(inner)  24.9 us
    another operation x4, other arithmetic, make_basis(): return jax.scipy.linalg.solve_triangular(lower, sketched.T, lower=True)  21 us
    all_to_all x1, blocking collectives, per_device(): lax.all_to_all(core_one, 'wide', split_axis=0, concat_axis=2, tiled=True)  12.1 us
  transfers between devices with their start and end apart: 2, of which 2 were waited for; matrix products, arithmetic and copies ran while one was open for 1% of the time, Pallas kernels for 0%

commit v1 on v0

--- a/solution.py
+++ b/solution.py
@@ -23,7 +23,10 @@
     highest = lax.Precision.HIGHEST
     basis_one = make_basis(field, sketch_one, ranks[0])
     core_one = jnp.einsum("rn,ykn->rky", basis_one, field, precision=highest)
-    regrouped = lax.all_to_all(core_one, "wide", split_axis=0, concat_axis=2, tiled=True)
+    regrouped = jnp.concatenate(
+        lax.all_to_all(jnp.stack(jnp.split(core_one, lax.axis_size("wide"), axis=0)), "wide", 0, 0),
+        axis=2,
+    )
     basis_two = make_basis(regrouped, sketch_two, ranks[1])
     return jnp.einsum("sn,rkn->rks", basis_two, regrouped, precision=highest)
 

time: 347 us -> 360 us (1.037)
  local copies, waits for them, and re-layouts: 5.47 us -> 19.2 us
    another operation x0 -> x35, local copies, waits for them, and re-layouts: none -> 7.9 us  [per_device(): jnp.stack(jnp.split(core_one, lax.axis_size('wide'), axis=0))]
    unnamed x10 -> x77, local copies, waits for them, and re-layouts: 3.02 us -> 9.14 us
where the time goes in v1:
time: 360 us
  waiting for transfers between devices  254 us (71%)
  other arithmetic  49.5 us (14%)
  local copies, waits for them, and re-layouts  19.2 us (5%)
  between operations  13.9 us (4%)
  blocking collectives  12.1 us (3%)
  matrix products  11.5 us (3%)
    psum x2, waiting for transfers between devices, combine(): return lax.psum(partial_sum, ('wide', 'narrow'))  254 us
    another operation x6, other arithmetic, make_basis(): lower = jnp.linalg.cholesky(inner)  24.8 us
    another operation x4, other arithmetic, make_basis(): return jax.scipy.linalg.solve_triangular(lower, sketched.T, lower=True)  20.9 us
    all_to_all x1, blocking collectives, per_device(): lax.all_to_all(jnp.stack(jnp.split(core_one, lax.axis_size('wide'), axis=...  12.1 us
    unnamed x77, local copies, waits for them, and re-layouts  9.14 us
    another operation x35, local copies, waits for them, and re-layouts, per_device(): jnp.stack(jnp.split(core_one, lax.axis_size('wide'), axis=0))  7.9 us
  transfers between devices with their start and end apart: 2, of which 2 were waited for; matrix products, arithmetic and copies ran while one was open for 1% of the time, Pallas kernels for 0%

profile of v1, /device:TPU:0, one launch (start us, length us, event | category | flops | bytes accessed | tf_op | source)
XLA Modules:
  0.0 359.9 jit_solution(6705686926650443269)
XLA Ops:
  6.5 1.1 copy-done
  7.6 2.9 convolution_bitcast_fusion
  11.8 0.7 broadcast_subtract_fusion.1
  12.4 0.7 compare_convert_fusion.1
  13.1 131.9 %all-reduce.3.cloned.1.call-done = f32[512,512]{1,0:T(8,128)} async-done(((f32[512,512]{1,0:T(8,128)}), f32[512,512]{1,0:T(8,128)}) %all-reduce.3.cloned.1.call-update) | async-done | bytes 1048592 | tf_op jit(solution)/shard_map/psum | solution.py:8
  145.1 2.2 fusion.6
  148.1 11.7 %cholesky.44 = f32[128,128]{1,0:T(8,128)S(1)} custom-call(f32[128,128]{1,0:T(8,128)S(1)} %copy.52), custom_call_target="Cholesky" | custom-call | tf_op jit(solution)/shard_map/jit(cholesky)/cholesky | solution.py:18
  159.9 0.7 compare_reduce_fusion.1
  161.2 9.8 %custom-call.10 = f32[1,128,128]{1,2,0:T(8,128)S(1)} custom-call(f32[1,128,128]{2,1,0:T(8,128)S(1)} %fusion.11), custom_call_target="InvertDiagBlocksLowerTriangular" | custom-call | tf_op jit(solution)/shard_map/jit(_solve_triangular)/triangular_solve | solution.py:19
  171.4 1.1 convolution_bitcast_fusion.3
  172.5 0.7 slice_bitcast_fusion.19
  173.2 2.8 slice_bitcast_fusion
  177.7 0.7 copy-done.18
  178.7 0.7 copy-done.16
  179.6 0.7 copy-done.14
  180.6 0.7 copy-done.12
  181.5 0.7 copy-done.10
  182.5 0.7 copy-done.8
  184.4 0.7 copy-done.4
  185.3 0.7 copy-done.2
  187.4 12.1 %all_to_all.5 = f32[32,1,1408]{2,1,0:T(1,128)S(1)} all-to-all(f32[32,1,1408]{2,1,0:T(1,128)S(1)} %reshape.47), channel_id=1, replica_groups=mesh['wide'=32,'narrow'=1] {'wide'}, dimensions={0} | all-to-all | bytes 360448 | tf_op jit(solution)/shard_map/all_to_all | solution.py:27
  200.1 1.1 reduce.4
  201.1 0.7 reshape.48
  201.8 1.3 convolution_bitcast_fusion.1
  203.2 0.7 broadcast_subtract_fusion
  204.5 121.8 %all-reduce.5.cloned.1.call-done = f32[256,256]{1,0:T(8,128)} async-done(((f32[256,256]{1,0:T(8,128)}), f32[256,256]{1,0:T(8,128)}) %all-reduce.5.cloned.1.call-update) | async-done | bytes 262160 | tf_op jit(solution)/shard_map/psum | solution.py:8
  326.3 1.3 fusion.8
  328.2 11.7 %cholesky.55 = f32[128,128]{1,0:T(8,128)S(1)} custom-call(f32[128,128]{1,0:T(8,128)S(1)} %copy.90), custom_call_target="Cholesky" | custom-call | tf_op jit(solution)/shard_map/jit(cholesky)/cholesky | solution.py:18
  340.6 0.7 fusion.12
  341.3 9.8 %custom-call.11 = f32[1,128,128]{1,2,0:T(8,128)S(1)} custom-call(f32[1,128,128]{2,1,0:T(8,128)S(1)} %fusion.12), custom_call_target="InvertDiagBlocksLowerTriangular" | custom-call | tf_op jit(solution)/shard_map/jit(_solve_triangular)/triangular_solve | solution.py:19
  351.4 1.0 fusion.1
  352.4 0.7 copy.92
  (121 shorter events, 11.8 us)
Async XLA Ops:
  6.5 1.1 copy-start
  6.5 138.5 %all-reduce.3.cloned.1.call-start = ((), (), s32[]{:S(2)}) async-start(), calls=%async_computation.1 | async-start | bytes 2097152 | tf_op jit(solution)/shard_map/psum | solution.py:8
  10.5 0.7 copy-start.21
  10.5 134.5 %copy-start.19 = (f32[512,128]{1,0:T(8,128)S(1)}, f32[512,128]{1,0:T(8,128)}, u32[]{:S(2)}) copy-start(f32[512,128]{1,0:T(8,128)} %param.6) | copy-start | bytes 786436
  10.6 315.7 %all-reduce.5.cloned.1.call-start = ((), (), s32[]{:S(2)}) async-start(), calls=%async_computation.2 | async-start | bytes 524288 | tf_op jit(solution)/shard_map/psum | solution.py:8
  177.5 0.9 copy-start.18
  177.6 1.0 copy-start.17
  178.4 0.9 copy-start.16
  178.6 0.9 copy-start.15
  179.3 0.9 copy-start.14
  179.5 0.9 copy-start.13
  180.3 0.9 copy-start.12
  180.5 0.9 copy-start.11
  181.2 0.9 copy-start.10
  181.4 0.9 copy-start.9
  182.2 0.9 copy-start.8
  182.4 0.9 copy-start.7
  183.2 0.9 copy-start.6
  183.3 0.9 copy-start.5
  184.1 0.9 copy-start.4
  184.3 0.9 copy-start.3
  185.1 0.9 copy-start.2
  185.2 0.9 copy-start.1
  203.1 123.1 %copy-start.20 = (f32[256,128]{1,0:T(8,128)S(1)}, f32[256,128]{1,0:T(8,128)}, u32[]{:S(2)}) copy-start(f32[256,128]{1,0:T(8,128)} %param.7) | copy-start | bytes 393220
Sparse Core Ops, SparseCore 0:
  12.5 132.4 all-reduce.2
  203.3 122.9 all-reduce.4

commit v2 on v0

--- a/solution.py
+++ b/solution.py
@@ -5,7 +5,7 @@
 
 
 def combine(partial_sum):
-    return lax.psum(partial_sum, ("wide", "narrow"))
+    return jnp.sum(lax.all_gather(partial_sum, ("wide", "narrow")), axis=0)
 
 
 def make_basis(local, sketch, rank):

time: 347 us -> 375 us (1.081)
  other arithmetic: 49.5 us -> 65.7 us
  waiting for transfers between devices: 254 us -> 269 us
    all_gather x0 -> x2, waiting for transfers between devices: none -> 269 us  [combine(): return jnp.sum(lax.all_gather(partial_sum, ('wide', 'narrow')), axis=0)]
    psum x2 -> x0, waiting for transfers between devices: 254 us -> none  [combine(): return lax.psum(partial_sum, ('wide', 'narrow'))]
    reduce_sum x0 -> x2, other arithmetic: none -> 16.2 us  [combine(): return jnp.sum(lax.all_gather(partial_sum, ('wide', 'narrow')), axis=0)]
where the time goes in v2:
time: 375 us
  waiting for transfers between devices  269 us (72%)
  other arithmetic  65.7 us (18%)
  between operations  13.6 us (4%)
  blocking collectives  11.3 us (3%)
  matrix products  9.29 us (2%)
  local copies, waits for them, and re-layouts  5.62 us (1%)
    all_gather x2, waiting for transfers between devices, combine(): return jnp.sum(lax.all_gather(partial_sum, ('wide', 'narrow')), axis=0)  269 us
    another operation x6, other arithmetic, make_basis(): lower = jnp.linalg.cholesky(inner)  24.9 us
    another operation x4, other arithmetic, make_basis(): return jax.scipy.linalg.solve_triangular(lower, sketched.T, lower=True)  21 us
    reduce_sum x2, other arithmetic, combine(): return jnp.sum(lax.all_gather(partial_sum, ('wide', 'narrow')), axis=0)  16.2 us
    all_to_all x1, blocking collectives, per_device(): lax.all_to_all(core_one, 'wide', split_axis=0, concat_axis=2, tiled=True)  11.3 us
  transfers between devices with their start and end apart: 2, of which 2 were waited for; matrix products, arithmetic and copies ran while one was open for 1% of the time, Pallas kernels for 0%

profile of v2, /device:TPU:0, one launch (start us, length us, event | category | flops | bytes accessed | tf_op | source)
XLA Modules:
  0.0 374.8 jit_solution(3805061560455757645)
XLA Ops:
  6.5 1.1 copy-done
  7.6 2.8 convolution_bitcast_fusion
  10.6 1.3 fusion.20
  11.9 0.6 compare_convert_fusion.1
  12.5 0.6 broadcast_subtract_fusion.1
  13.2 195.0 %all-gather.5.cloned.1.call-done = f32[16384,512]{1,0:T(8,128)} async-done(((f32[512,512]{1,0:T(8,128)}), f32[16384,512]{1,0:T(8,128)}) %all-gather.5.cloned.1.call-update) | async-done | bytes 33554448 | tf_op jit(solution)/shard_map/all_gather | solution.py:8
  208.2 12.3 %reduce_sum.18 = f32[512,512]{1,0:T(8,128)S(1)} reduce(f32[32,512,512]{2,1,0:T(8,128)} %bitcast.54, f32[]{:T(128)} %constant.43.clone.1), dimensions={0}, to_apply=%region_0.0 | reduce | flops 8126464 | bytes 34603012 | tf_op jit(solution)/shard_map/reduce_sum | solution.py:8
  220.4 1.0 fusion.6
  221.4 0.6 convolution_add_fusion.1
  222.2 11.7 %cholesky.44 = f32[128,128]{1,0:T(8,128)S(1)} custom-call(f32[128,128]{1,0:T(8,128)S(1)} %copy.28), custom_call_target="Cholesky" | custom-call | tf_op jit(solution)/shard_map/jit(cholesky)/cholesky | solution.py:18
  234.0 0.7 compare_reduce_fusion.1
  234.7 0.7 fusion.11
  235.4 9.8 %custom-call.10 = f32[1,128,128]{1,2,0:T(8,128)S(1)} custom-call(f32[1,128,128]{2,1,0:T(8,128)S(1)} %fusion.11), custom_call_target="InvertDiagBlocksLowerTriangular" | custom-call | tf_op jit(solution)/shard_map/jit(_solve_triangular)/triangular_solve | solution.py:19
  245.2 0.4 convolution_bitcast_fusion.2
  245.7 1.1 convolution_bitcast_fusion.3
  247.0 0.6 reshape.41
  247.6 11.3 %all_to_all.18 = f32[32,1,1408]{2,1,0:T(1,128)S(1)} all-to-all(f32[32,1,1408]{2,1,0:T(1,128)S(1)} %reshape.41), channel_id=1, replica_groups=mesh['wide'=32,'narrow'=1] {'wide'}, dimensions={0} | all-to-all | bytes 360448 | tf_op jit(solution)/shard_map/all_to_all | solution.py:26
  258.9 0.6 broadcast.90
  259.5 1.1 reduce.4
  260.6 0.7 reshape.42
  261.3 1.3 convolution_bitcast_fusion.1
  262.7 0.7 compare_convert_fusion
  263.4 0.7 broadcast_subtract_fusion
  264.0 74.2 %all-gather.7.cloned.1.call-done = f32[8192,256]{1,0:T(8,128)} async-done(((f32[256,256]{1,0:T(8,128)}), f32[8192,256]{1,0:T(8,128)}) %all-gather.7.cloned.1.call-update) | async-done | bytes 8388624 | tf_op jit(solution)/shard_map/all_gather | solution.py:8
  338.2 3.9 %reduce_sum.19 = f32[256,256]{1,0:T(8,128)S(1)} reduce(f32[32,256,256]{2,1,0:T(8,128)} %bitcast.55, f32[]{:T(128)} %constant.43.clone.1), dimensions={0}, to_apply=%region_3.5 | reduce | flops 2031616 | bytes 8650756 | tf_op jit(solution)/shard_map/reduce_sum | solution.py:8
  342.5 0.4 convolution_add_fusion
  343.1 11.7 %cholesky.55 = f32[128,128]{1,0:T(8,128)S(1)} custom-call(f32[128,128]{1,0:T(8,128)S(1)} %copy.35), custom_call_target="Cholesky" | custom-call | tf_op jit(solution)/shard_map/jit(cholesky)/cholesky | solution.py:18
  354.9 0.6 compare_reduce_fusion
  355.5 0.7 fusion.12
  356.2 9.8 %custom-call.11 = f32[1,128,128]{1,2,0:T(8,128)S(1)} custom-call(f32[1,128,128]{2,1,0:T(8,128)S(1)} %fusion.12), custom_call_target="InvertDiagBlocksLowerTriangular" | custom-call | tf_op jit(solution)/shard_map/jit(_solve_triangular)/triangular_solve | solution.py:19
  366.3 1.0 fusion.1
  367.3 0.7 copy.37
  (20 shorter events, 1.5 us)
Async XLA Ops:
  6.5 1.1 copy-start
  6.5 213.9 %copy-start.1 = (f32[512,128]{1,0:T(8,128)S(1)}, f32[512,128]{1,0:T(8,128)}, u32[]{:S(2)}) copy-start(f32[512,128]{1,0:T(8,128)} %param.6) | copy-start | bytes 786436
  6.5 335.6 %copy-start.2 = (f32[256,128]{1,0:T(8,128)S(1)}, f32[256,128]{1,0:T(8,128)}, u32[]{:S(2)}) copy-start(f32[256,128]{1,0:T(8,128)} %param.7) | copy-start | bytes 393220
  6.5 201.6 %all-gather.5.cloned.1.call-start = ((), (), s32[]{:S(2)}) async-start(), calls=%async_computation.1 | async-start | bytes 34603008 | tf_op jit(solution)/shard_map/all_gather | solution.py:8
  10.5 327.7 %all-gather.7.cloned.1.call-start = ((), (), s32[]{:S(2)}) async-start(), calls=%async_computation.2 | async-start | bytes 8650752 | tf_op jit(solution)/shard_map/all_gather | solution.py:8
Sparse Core Ops, SparseCore 0:
  10.6 197.4 all-gather.4
  262.8 75.3 all-gather.6
